TPU v7x, 128 devices: a whole 4x4x4 slice. The times are simulated.
128 devices in a mesh: tok: 4 (over z), code: 32 (over x, y, core).
Axes of the slice: x: 4, y: 4, z: 4, core: 2. Of those that a mesh axis runs over, the one named last changes fastest.
Arguments:
- tokens: float32 [65536, 256], P(('tok', 'code')), may hold values from -14 to 14
- codebook: float32 [8192, 256], P('code'), may hold values from -6 to 6
Outputs:
- centroids: float32 [8192, 256], P('code')
- counts: float32 [8192], P('code')
All inputs are finite; a program needn't handle non-finite values.
Results may differ from a plain program's by a relative error of at most 0.0003.
Values sent between devices are 32-bit elements; how exact they have to be, the bound alone decides.
A program may use at most 128 MiB of HBM per device.

v0:
```python
import functools
import math

import jax
import jax.numpy as jnp
from jax import lax
from jax.experimental import pallas as pl
from jax.experimental.pallas import tpu as pltpu
from jax.sharding import PartitionSpec as P

MESH = pl.DeviceIdType.MESH
F32, BF16 = jnp.float32, jnp.bfloat16
ITERS = 2
PRIOR_WEIGHT = 1.0
N = 4
CORES = 2
GROUP = N * CORES
D = 256
FRAMES = 512
OWNED = 256
HALF = OWNED // N // 2
BLOCK = N * HALF
BLOCKS = 2 * N
TILES = GROUP
TILE = FRAMES
PIECES = 4
ROWS = FRAMES // PIECES
BATCH = 4
BATCHES = TILES // BATCH
SUMS = BLOCK + 8
SHARPNESS = math.log2(math.e) / math.sqrt(D)
LAST = (((1,), (1,)), ((), ()))


def split(value):
    high = value.astype(BF16)
    return high, (value - high.astype(F32)).astype(BF16)


def em_kernel(
    frames, codebook, cent_out, count_out,
    tok, thi, tlo, tnorm, cod, chi, clo, cnorm, scores, tops, top, total, lognorm, stats, part, rs1, mid, rs2, fin, flip,
    own_sem, tok_send, tok_recv, share_send, share_recv, c1_send, c1_recv, c2_send, c2_recv, st_send, st_recv,
    r1_send, r1_recv, r2_send, r2_recv, f_send, f_recv,
):
    z = lax.axis_index("tok")
    place = lax.axis_index("code")
    core = lax.rem(place, CORES)
    y = lax.rem(place // CORES, N)
    x = place // (CORES * N)
    mine = core * N + z

    def at(pz, px, py, pc):
        return (pz, (px * N + py) * CORES + pc)

    def ahead(p, o):
        return lax.rem(p + o, N)

    def remote(src, dst, send_sem, recv_sem, device):
        return pltpu.make_async_remote_copy(
            src_ref=src, dst_ref=dst, send_sem=send_sem, recv_sem=recv_sem, device_id=device, device_id_type=MESH
        )

    def await_bytes(ref, sem):
        pltpu.make_async_copy(ref, ref, sem).wait()

    def group_peer(j):
        peer = lax.rem(mine + j, GROUP)
        return at(lax.rem(peer, N), x, y, peer // N)

    barrier = pltpu.get_barrier_semaphore()
    peers = [at(z, ahead(x, o), y, core) for o in range(1, N)]
    peers += [at(z, x, ahead(y, o), core) for o in range(1, N)]
    peers += [group_peer(j) for j in range(1, GROUP)]
    for peer in peers:
        pl.semaphore_signal(barrier, inc=1, device_id=peer, device_id_type=MESH)
    pl.semaphore_wait(barrier, len(peers))

    def block_of(half, o):
        return ahead(y, o) if half == 0 else N + ahead(x, o)

    def across(half, o):
        return at(z, ahead(x, o), y, core) if half == 0 else at(z, x, ahead(y, o), core)

    def along(half, o):
        return at(z, x, ahead(y, o), core) if half == 0 else at(z, ahead(x, o), y, core)

    slot = (x, y)

    def start_stage1(it, half, src):
        dst = cod.at[it, block_of(half, 0), slot[half]]
        for o in (2, 1, 3):
            remote(src, dst, c1_send.at[it, half, o - 1], c1_recv.at[it, half, o - 1], across(half, o)).start()

    def await_stage1(it, half):
        for o in range(1, N):
            await_bytes(cod.at[it, 0, 0], c1_recv.at[it, half, o - 1])

    def start_stage2(it, half):
        block = cod.at[it, block_of(half, 0)]
        for o in (1, 3, 2):
            remote(block, block, c2_send.at[it, half, o - 1], c2_recv.at[it, half, o - 1], along(half, o)).start()

    def await_block(it, half, o):
        await_bytes(cod.at[it, 0], c2_recv.at[it, half, N - 1 - o])

    before, after, opposite = ahead(z, N - 1), ahead(z, 1), ahead(z, 2)
    first, other = core * N, (1 - core) * N
    next_device, last_device = at(after, x, y, core), at(before, x, y, core)

    def rows_of(p, part=0, parts=1):
        return pl.ds(p * ROWS + part * (ROWS // parts), ROWS // parts)

    def direct(p):
        src, dst = frames.at[rows_of(p)], tok.at[first + z, rows_of(p)]
        remote(src, dst, tok_send.at[p, 0], tok_recv.at[p, 0], next_device).start()
        remote(src, dst, tok_send.at[p, 1], tok_recv.at[p, 1], last_device).start()

    def forward(p):
        await_bytes(tok.at[0, rows_of(p)], tok_recv.at[p, 0])
        low = tok.at[first + before, rows_of(p, 0, 2)]
        remote(low, low, tok_send.at[p, 2], tok_recv.at[p, 2], next_device).start()
        await_bytes(tok.at[0, rows_of(p)], tok_recv.at[p, 1])
        high = tok.at[first + after, rows_of(p, 1, 2)]
        remote(high, high, tok_send.at[p, 3], tok_recv.at[p, 3], last_device).start()

    def await_forwarded():
        for p in range(PIECES):
            await_bytes(tok.at[0, rows_of(p, 0, 2)], tok_recv.at[p, 2])
            await_bytes(tok.at[0, rows_of(p, 1, 2)], tok_recv.at[p, 3])

    def share(i, src, place):
        remote(src, tok.at[first + place], share_send.at[i], share_recv.at[i], at(z, x, y, 1 - core)).start()

    def await_shared(i):
        await_bytes(tok.at[0], share_recv.at[i])

    own_codes = [codebook.at[z, half] for half in range(2)]
    keep = [
        pltpu.make_async_copy(own_codes[0], cod.at[0, y, x], own_sem.at[0]),
        pltpu.make_async_copy(own_codes[1], cod.at[0, N + x, y], own_sem.at[1]),
        pltpu.make_async_copy(frames, tok.at[first + z], own_sem.at[2]),
    ]
    for half in range(2):
        start_stage1(0, half, own_codes[half])
    for copy in keep:
        copy.start()
    for p in range(PIECES):
        direct(p)
    share(0, frames, z)
    for copy in keep:
        copy.wait()
    for half in range(2):
        await_stage1(0, half)
        start_stage2(0, half)
    forward(0)
    forward(1)
    for half in range(2):
        for o in range(1, N):
            await_block(0, half, o)

    def parts_of(codes):
        norms = jnp.sum(codes * codes, axis=1, keepdims=True) * SHARPNESS
        return *split(codes * (2.0 * SHARPNESS)), jnp.broadcast_to(norms, (codes.shape[0], 128))

    def split_block(b, _):
        chi[b], clo[b], cnorm[b] = parts_of(cod[0, b].reshape(BLOCK, D))
        return 0

    lax.fori_loop(0, BLOCKS, split_block, 0)

    def score(high, low, norms, g):
        inner = lax.dot_general(
            jnp.concatenate([high, high, low], axis=1),
            jnp.concatenate([thi[g], tlo[g], thi[g]], axis=1),
            LAST,
            preferred_element_type=F32,
        )
        return inner - jnp.tile(norms, (1, TILE // 128))

    def add_up(g, tiles, carry):
        old_top, old_total = carry if carry is not None else (None, None)
        new_top = tops[g] if carry is None else jnp.maximum(old_top, tops[g])
        new_total = None if carry is None else old_total * jnp.exp2(old_top - new_top)
        for tile in tiles:
            more = jnp.sum(jnp.exp2(tile - new_top), axis=0, keepdims=True)
            new_total = more if new_total is None else new_total + more
        return new_top, new_total

    def publish(it, g, row_top, row_total):
        norm = tnorm[g]
        shift = (row_top - norm) + norm
        stats[it, g // BATCH, mine, g % BATCH] = shift + jnp.log2(row_total * jnp.exp2(row_top - shift))

    def send_stats(it, batch):
        own = stats.at[it, batch, mine]
        for j in range(1, GROUP):
            remote(own, own, st_send.at[it, batch], st_recv.at[it, batch], group_peer(j)).start()

    def normalise(it, batch):
        await_bytes(stats.at[it, batch, pl.ds(0, GROUP - 1)], st_recv.at[it, batch])
        for q in range(BATCH):
            g = batch * BATCH + q
            logs = stats[it, batch, :, q, 0, :]
            highest = jnp.max(logs, axis=0, keepdims=True)
            lognorm[g] = highest + jnp.log2(jnp.sum(jnp.exp2(logs - highest), axis=0, keepdims=True))

    def score_tile(g):
        tile = tok[g]
        thi[g], tlo[g] = split(tile)
        squares = tile * tile
        squares = squares[:, :128] + squares[:, 128:]
        tnorm[g] = jnp.sum(squares.T, axis=0, keepdims=True) * SHARPNESS
        high, low = chi[...].reshape(BLOCKS * BLOCK, D), clo[...].reshape(BLOCKS * BLOCK, D)
        tile_scores = score(high, low, cnorm[...].reshape(BLOCKS * BLOCK, 128), g)
        scores[:, g] = tile_scores.reshape(BLOCKS, BLOCK, TILE)
        tops[g] = jnp.max(tile_scores, axis=0, keepdims=True)

    def sum_tile(g):
        publish(0, g, *add_up(g, [scores[:, g].reshape(BLOCKS * BLOCK, TILE)], None))

    def source(i):
        place = jnp.where(i < 2, z, jnp.where(i < 6, jnp.where(i % 2 == 0, before, after), opposite))
        ours = (i == 0) | (i == 2) | (i == 3)
        return jnp.where(i < 6, jnp.where(ours, core, 1 - core), i - 6) * N + place

    def move_on(i):
        @pl.when(i == 1)
        def _():
            forward(2)
            await_shared(0)

        @pl.when(i == 2)
        def _():
            forward(3)
            share(1, tok.at[first + before], before)
            share(2, tok.at[first + after], after)

        @pl.when(i == 4)
        def _():
            await_shared(1)

        @pl.when(i == 5)
        def _():
            await_shared(2)

        @pl.when(i == 6)
        def _():
            await_forwarded()
            share(3, tok.at[first + opposite], opposite)
            await_shared(3)

    score_tile(source(0))

    def step(i, _):
        move_on(i)
        sum_tile(source(i - 1))
        score_tile(source(i))

        @pl.when(i == TILES - 1)
        def _():
            send_stats(0, 0)

        return 0

    lax.fori_loop(1, TILES, step, 0)
    sum_tile(source(TILES - 1))
    send_stats(0, 1)

    def gray(i):
        return jnp.bitwise_xor(i, i // 2)

    def weigh(blocks, batch):
        lefts, rights, counts = [], [], None
        for q in range(BATCH):
            g = batch * BATCH + q
            pair_scores = jnp.concatenate([scores[b, g] for b in blocks], axis=0)
            weights = jnp.exp2(pair_scores - lognorm[g])
            for c in range(TILE // 128):
                piece = weights[:, c * 128 : (c + 1) * 128]
                counts = piece if counts is None else counts + piece
            high, low = split(weights)
            lefts += [high, high, low]
            rights += [thi[g], tlo[g], thi[g]]
        weighted = jnp.dot(jnp.concatenate(lefts, axis=1), jnp.concatenate(rights, axis=0), preferred_element_type=F32)
        for half in range(2):
            part[blocks[half], pl.ds(0, BLOCK)] += weighted[half * BLOCK : (half + 1) * BLOCK]
            row = jnp.sum(counts[half * BLOCK : (half + 1) * BLOCK].T, axis=0, keepdims=True)
            part[blocks[half], pl.ds(BLOCK, 8)] += jnp.broadcast_to(jnp.tile(row, (1, 2)), (8, D))

    def moments(it):
        part[...] = jnp.zeros_like(part)
        normalise(it, 0)

        def step(i, _):
            o, batch = gray(N - 1 - i // BATCHES), i % BATCHES

            @pl.when(i == 1)
            def _():
                normalise(it, 1)

            blocks = [block_of(half, o) for half in range(2)]
            weigh(blocks, batch)

            @pl.when((batch == BATCHES - 1) & (o != 0))
            def _():
                for half in range(2):
                    remote(
                        part.at[blocks[half]], rs1.at[it, half, o - 1], r1_send.at[it, half, o - 1], r1_recv.at[it, half, o - 1], along(half, o)
                    ).start()

            return 0

        lax.fori_loop(0, N * BATCHES, step, 0)

    def reduce_sums(it, use):
        for half in range(2):
            for o in range(1, N):
                await_bytes(part.at[0], r1_recv.at[it, half, o - 1])
            row = part[block_of(half, 0)] + rs1[it, half, 0] + rs1[it, half, 1] + rs1[it, half, 2]
            for p in range(N):
                mid[half, p, pl.ds(0, HALF)] = row[p * HALF : (p + 1) * HALF]
                mid[half, p, pl.ds(HALF, 8)] = row[BLOCK:]
            for o in (2, 1, 3):
                remote(
                    mid.at[half, ahead(slot[half], o)], rs2.at[it, half, o - 1], r2_send.at[it, half, o - 1], r2_recv.at[it, half, o - 1], across(half, o)
                ).start()
        for half in range(2):
            for o in range(1, N):
                await_bytes(mid.at[0, 0], r2_recv.at[it, half, o - 1])
            sums = mid[half, slot[half]] + rs2[it, half, 0] + rs2[it, half, 1] + rs2[it, half, 2]
            flip[half] = jnp.broadcast_to(sums[HALF : HALF + 1, :128], (128, 128)).T
            count = flip[half, pl.ds(pl.multiple_of(slot[half] * HALF, HALF), HALF)]
            old = cod[it, block_of(half, 0), slot[half]]
            use(half, (sums[:HALF] + PRIOR_WEIGHT * old) / (jnp.tile(count, (1, 2)) + PRIOR_WEIGHT), count)

    def sent(it):
        for half in range(2):
            for o in range(1, N):
                await_bytes(part.at[0], r1_send.at[it, half, o - 1])
                await_bytes(mid.at[0, 0], r2_send.at[it, half, o - 1])

    def next_codes(half, codes, _):
        cod[1, block_of(half, 0), slot[half]] = codes
        start_stage1(1, half, cod.at[1, block_of(half, 0), slot[half]])

    moments(0)
    reduce_sums(0, next_codes)
    for half in range(2):
        await_stage1(1, half)
        start_stage2(1, half)

    def score_pair(o):
        blocks = [block_of(half, o) for half in range(2)]
        codes = jnp.concatenate([cod[1, b].reshape(BLOCK, D) for b in blocks], axis=0)
        high, low, norms = parts_of(codes)
        for g in range(TILES):
            tile_scores = score(high, low, norms, g)
            for half in range(2):
                scores[blocks[half], g] = tile_scores[half * BLOCK : (half + 1) * BLOCK]
            tops[g] = jnp.max(tile_scores, axis=0, keepdims=True)

    def sum_pair(o, g):
        blocks = [block_of(half, o) for half in range(2)]
        return add_up(g, [scores[b, g] for b in blocks], (top[g], total[g]))

    top[...] = jnp.full_like(top, -1e30)
    total[...] = jnp.zeros_like(total)
    score_pair(0)

    def pair_step(i, _):
        o, previous = gray(i), gray(i - 1)
        for half in range(2):
            await_block(1, half, o)
        for g in range(TILES):
            top[g], total[g] = sum_pair(previous, g)
        score_pair(o)
        return 0

    lax.fori_loop(1, N, pair_step, 0)

    def last_sum(batch, _):
        for q in range(BATCH):
            g = batch * BATCH + q
            publish(1, g, *sum_pair(N // 2, g))
        send_stats(1, batch)
        return 0

    lax.fori_loop(0, BATCHES, last_sum, 0)
    sent(0)
    moments(1)

    def last_codes(half, codes, count):
        fin[z, pl.ds(half * HALF, HALF)] = codes
        flip[2, pl.ds(half * HALF, HALF)] = count

    flip[2] = jnp.zeros((128, 128), F32)
    reduce_sums(1, last_codes)
    fin[z, pl.ds(2 * HALF, 8)] = jnp.tile(flip[2].T[:8], (1, 2))
    for o in (2, 1, 3):
        remote(fin.at[z], fin.at[z], f_send.at[o - 1], f_recv.at[o - 1], at(ahead(z, o), x, y, core)).start()
    sent(1)

    for p in range(PIECES):
        for i in range(2):
            await_bytes(tok.at[0, rows_of(p)], tok_send.at[p, i])
            await_bytes(tok.at[0, rows_of(p, 0, 2)], tok_send.at[p, 2 + i])
    for i in range(4):
        await_bytes(tok.at[0], share_send.at[i])
    for it in range(ITERS):
        for batch in range(BATCHES):
            await_bytes(stats.at[it, batch, pl.ds(0, GROUP - 1)], st_send.at[it, batch])
        for half in range(2):
            for o in range(1, N):
                await_bytes(cod.at[it, 0, 0], c1_send.at[it, half, o - 1])
                await_bytes(cod.at[it, 0], c2_send.at[it, half, o - 1])
    for o in range(1, N):
        await_bytes(fin.at[0], f_send.at[o - 1])
        await_bytes(fin.at[0], f_recv.at[o - 1])
    for p in range(N):
        cent_out[pl.ds(p * 2 * HALF, 2 * HALF)] = fin[p, pl.ds(0, 2 * HALF)]
        count_out[:, pl.ds(p * 2 * HALF, 2 * HALF)] = fin[p, pl.ds(2 * HALF, 1), pl.ds(0, 2 * HALF)]


def on_device(tokens, codebook):
    vmem, dma = pltpu.VMEM, pltpu.SemaphoreType.DMA
    peers = N - 1
    centroids, counts = pl.pallas_call(
        em_kernel,
        out_shape=[jax.ShapeDtypeStruct((OWNED, D), F32), jax.ShapeDtypeStruct((1, OWNED), F32)],
        in_specs=[pl.BlockSpec(memory_space=pl.ANY)] * 2,
        out_specs=[pl.BlockSpec(memory_space=vmem)] * 2,
        scratch_shapes=[
            vmem((TILES, TILE, D), F32),
            vmem((TILES, TILE, D), BF16),
            vmem((TILES, TILE, D), BF16),
            vmem((TILES, 1, TILE), F32),
            vmem((ITERS, BLOCKS, N, HALF, D), F32),
            vmem((BLOCKS, BLOCK, D), BF16),
            vmem((BLOCKS, BLOCK, D), BF16),
            vmem((BLOCKS, BLOCK, 128), F32),
            vmem((BLOCKS, TILES, BLOCK, TILE), F32),
            vmem((TILES, 1, TILE), F32),
            vmem((TILES, 1, TILE), F32),
            vmem((TILES, 1, TILE), F32),
            vmem((TILES, 1, TILE), F32),
            vmem((ITERS, BATCHES, GROUP, BATCH, 1, TILE), F32),
            vmem((BLOCKS, SUMS, D), F32),
            vmem((ITERS, 2, peers, SUMS, D), F32),
            vmem((2, N, HALF + 8, D), F32),
            vmem((ITERS, 2, peers, HALF + 8, D), F32),
            vmem((N, 2 * HALF + 8, D), F32),
            vmem((3, 128, 128), F32),
            dma((3,)),
            dma((PIECES, 4)),
            dma((PIECES, 4)),
            dma((4,)),
            dma((4,)),
            dma((ITERS, 2, peers)),
            dma((ITERS, 2, peers)),
            dma((ITERS, 2, peers)),
            dma((ITERS, 2, peers)),
            dma((ITERS, BATCHES)),
            dma((ITERS, BATCHES)),
            dma((ITERS, 2, peers)),
            dma((ITERS, 2, peers)),
            dma((ITERS, 2, peers)),
            dma((ITERS, 2, peers)),
            dma((peers,)),
            dma((peers,)),
        ],
        compiler_params=pltpu.CompilerParams(collective_id=0, has_side_effects=True, vmem_limit_bytes=56 << 20),
        cost_estimate=pl.CostEstimate(
            flops=ITERS * 2 * 3 * 2 * TILES * TILE * BLOCKS * BLOCK * D,
            bytes_accessed=4 * (FRAMES + 2 * OWNED) * D,
            transcendentals=ITERS * 2 * TILES * TILE * BLOCKS * BLOCK,
        ),
    )(tokens, codebook.reshape(N, 2, HALF, D))
    return centroids, counts.reshape(OWNED)


def solution(mesh):
    return jax.shard_map(
        on_device,
        mesh=mesh,
        in_specs=(P(("tok", "code"), None), P("code", None)),
        out_specs=(P("code", None), P("code")),
        check_vma=False,
    )
```

profile of v0, /device:TPU:0, one launch (start us, length us, event | category | flops | bytes accessed | tf_op | source)
XLA Modules:
  0.0 97.1 jit_solution(6195664850645992043)
XLA Ops:
  0.6 94.2 %shard_map.41 = (f32[256,256]{1,0:T(8,128)}, f32[1,256]{1,0:T(1,128)}) custom-call(f32[512,256]{1,0:T(8,128)} %frames.1, f32[4,2,32,256]{3,2,1,0:T(8,128)} %bitcast.3), custom_call_target="tpu_custom_call" | custom-call | flops 25769803776 | bytes 1048576 | tf_op jit(solution)/shard_map/pallas_call | solution.py:428
  94.8 0.0 copy-start
  94.8 1.7 %copy.6 = f32[256,256]{1,0:T(8,128)} copy(f32[256,256]{1,0:T(8,128)} %get-tuple-element.8) | data formatting | bytes 524288
  96.5 0.0 copy-done
  96.5 0.6 copy.7
Async XLA Ops:
  94.8 1.7 %copy-start = (f32[1,256]{1,0:T(1,128)S(1)}, f32[1,256]{1,0:T(1,128)}, u32[]{:S(2)}) copy-start(f32[1,256]{1,0:T(1,128)} %get-tuple-element.5) | copy-start | bytes 3076
where the time goes:
time: 97.2 us; the launch traced here: 97.1 us
  Pallas kernels  94.2 us (97%)
  local copies, waits for them, and re-layouts  2.24 us (2%)
    pallas_call x1, Pallas kernels, on_device(): pl.pallas_call(em_kernel, out_shape=[jax.ShapeDtypeStruct((OWNED, D), F32...  94.2 us
    unnamed x4, local copies, waits for them, and re-layouts  2.24 us

commit v1 on v0

--- a/solution.py
+++ b/solution.py
@@ -96,9 +96,9 @@
         for o in range(1, N):
             await_bytes(cod.at[it, 0, 0], c1_recv.at[it, half, o - 1])
 
-    def start_stage2(it, half):
+    def start_stage2(it, half, places):
         block = cod.at[it, block_of(half, 0)]
-        for o in (1, 3, 2):
+        for o in places:
             remote(block, block, c2_send.at[it, half, o - 1], c2_recv.at[it, half, o - 1], along(half, o)).start()
 
     def await_block(it, half, o):
@@ -152,7 +152,7 @@
         copy.wait()
     for half in range(2):
         await_stage1(0, half)
-        start_stage2(0, half)
+        start_stage2(0, half, (1, 3, 2))
     forward(0)
     forward(1)
     for half in range(2):
@@ -270,10 +270,9 @@
     def gray(i):
         return jnp.bitwise_xor(i, i // 2)
 
-    def weigh(blocks, batch):
+    def weigh(blocks, tiles):
         lefts, rights, counts = [], [], None
-        for q in range(BATCH):
-            g = batch * BATCH + q
+        for g in tiles:
             pair_scores = jnp.concatenate([scores[b, g] for b in blocks], axis=0)
             weights = jnp.exp2(pair_scores - lognorm[g])
             for c in range(TILE // 128):
@@ -289,20 +288,26 @@
             part[blocks[half], pl.ds(BLOCK, 8)] += jnp.broadcast_to(jnp.tile(row, (1, 2)), (8, D))
 
     def moments(it):
+        batches = BATCHES if it == 0 else 1
         part[...] = jnp.zeros_like(part)
         normalise(it, 0)
+        if batches == 1:
+            normalise(it, 1)
 
         def step(i, _):
-            o, batch = gray(N - 1 - i // BATCHES), i % BATCHES
-
-            @pl.when(i == 1)
-            def _():
-                normalise(it, 1)
+            o, batch = gray(N - 1 - i // batches), i % batches
+
+            if batches > 1:
+
+                @pl.when(i == 1)
+                def _():
+                    normalise(it, 1)
 
             blocks = [block_of(half, o) for half in range(2)]
-            weigh(blocks, batch)
-
-            @pl.when((batch == BATCHES - 1) & (o != 0))
+            size = TILES // batches
+            weigh(blocks, [batch * size + q for q in range(size)])
+
+            @pl.when((batch == batches - 1) & (o != 0))
             def _():
                 for half in range(2):
                     remote(
@@ -311,7 +316,7 @@
 
             return 0
 
-        lax.fori_loop(0, N * BATCHES, step, 0)
+        lax.fori_loop(0, N * batches, step, 0)
 
     def reduce_sums(it, use):
         for half in range(2):
@@ -348,7 +353,7 @@
     reduce_sums(0, next_codes)
     for half in range(2):
         await_stage1(1, half)
-        start_stage2(1, half)
+        start_stage2(1, half, (1, 3))
 
     def score_pair(o):
         blocks = [block_of(half, o) for half in range(2)]
@@ -367,6 +372,8 @@
     top[...] = jnp.full_like(top, -1e30)
     total[...] = jnp.zeros_like(total)
     score_pair(0)
+    for half in range(2):
+        start_stage2(1, half, (2,))
 
     def pair_step(i, _):
         o, previous = gray(i), gray(i - 1)

time: 97.2 us -> 96.4 us (level)
  no operation moved by 1% of the time
where the time goes in v1:
time: 96.4 us; the launch traced here: 96.3 us
  Pallas kernels  93.4 us (97%)
  local copies, waits for them, and re-layouts  2.24 us (2%)
    pallas_call x1, Pallas kernels, on_device(): pl.pallas_call(em_kernel, out_shape=[jax.ShapeDtypeStruct((OWNED, D), F32...  93.4 us
    unnamed x4, local copies, waits for them, and re-layouts  2.24 us

profile of v1, /device:TPU:0, one launch (start us, length us, event | category | flops | bytes accessed | tf_op | source)
XLA Modules:
  0.0 96.3 jit_solution(7669704842992557629)
XLA Ops:
  0.6 93.4 %shard_map.41 = (f32[256,256]{1,0:T(8,128)}, f32[1,256]{1,0:T(1,128)}) custom-call(f32[512,256]{1,0:T(8,128)} %frames.1, f32[4,2,32,256]{3,2,1,0:T(8,128)} %bitcast.3), custom_call_target="tpu_custom_call" | custom-call | flops 25769803776 | bytes 1048576 | tf_op jit(solution)/shard_map/pallas_call | solution.py:435
  94.0 0.0 copy-start
  94.0 1.7 %copy.6 = f32[256,256]{1,0:T(8,128)} copy(f32[256,256]{1,0:T(8,128)} %get-tuple-element.8) | data formatting | bytes 524288
  95.7 0.0 copy-done
  95.7 0.6 copy.7
Async XLA Ops:
  94.0 1.7 %copy-start = (f32[1,256]{1,0:T(1,128)S(1)}, f32[1,256]{1,0:T(1,128)}, u32[]{:S(2)}) copy-start(f32[1,256]{1,0:T(1,128)} %get-tuple-element.5) | copy-start | bytes 3076

commit v2 on v1

--- a/solution.py
+++ b/solution.py
@@ -206,17 +206,16 @@
             lognorm[g] = highest + jnp.log2(jnp.sum(jnp.exp2(logs - highest), axis=0, keepdims=True))
 
     def score_tile(g):
-        tile = tok[g]
-        thi[g], tlo[g] = split(tile)
-        squares = tile * tile
-        squares = squares[:, :128] + squares[:, 128:]
-        tnorm[g] = jnp.sum(squares.T, axis=0, keepdims=True) * SHARPNESS
+        thi[g], tlo[g] = split(tok[g])
         high, low = chi[...].reshape(BLOCKS * BLOCK, D), clo[...].reshape(BLOCKS * BLOCK, D)
         tile_scores = score(high, low, cnorm[...].reshape(BLOCKS * BLOCK, 128), g)
         scores[:, g] = tile_scores.reshape(BLOCKS, BLOCK, TILE)
         tops[g] = jnp.max(tile_scores, axis=0, keepdims=True)
 
     def sum_tile(g):
+        squares = tok[g] * tok[g]
+        squares = squares[:, :128] + squares[:, 128:]
+        tnorm[g] = jnp.sum(squares.T, axis=0, keepdims=True) * SHARPNESS
         publish(0, g, *add_up(g, [scores[:, g].reshape(BLOCKS * BLOCK, TILE)], None))
 
     def source(i):
@@ -429,12 +428,18 @@
         count_out[:, pl.ds(p * 2 * HALF, 2 * HALF)] = fin[p, pl.ds(2 * HALF, 1), pl.ds(0, 2 * HALF)]
 
 
+def hand_on(cent, count, cent_out, count_out):
+    cent_out[...] = cent[...]
+    count_out[...] = count[...]
+
+
 def on_device(tokens, codebook):
     vmem, dma = pltpu.VMEM, pltpu.SemaphoreType.DMA
     peers = N - 1
+    results = [jax.ShapeDtypeStruct((OWNED, D), F32), jax.ShapeDtypeStruct((1, OWNED), F32)]
     centroids, counts = pl.pallas_call(
         em_kernel,
-        out_shape=[jax.ShapeDtypeStruct((OWNED, D), F32), jax.ShapeDtypeStruct((1, OWNED), F32)],
+        out_shape=results,
         in_specs=[pl.BlockSpec(memory_space=pl.ANY)] * 2,
         out_specs=[pl.BlockSpec(memory_space=vmem)] * 2,
         scratch_shapes=[
@@ -483,6 +488,12 @@
             transcendentals=ITERS * 2 * TILES * TILE * BLOCKS * BLOCK,
         ),
     )(tokens, codebook.reshape(N, 2, HALF, D))
+    centroids, counts = pl.pallas_call(
+        hand_on,
+        out_shape=results,
+        in_specs=[pl.BlockSpec(memory_space=vmem)] * 2,
+        out_specs=[pl.BlockSpec(memory_space=vmem)] * 2,
+    )(centroids, counts)
     return centroids, counts.reshape(OWNED)
 
 

time: 96.4 us -> 95.7 us (level)
  local copies, waits for them, and re-layouts: 2.24 us -> 0 us
  Pallas kernels: 93.4 us -> 95 us
    unnamed x4 -> x0, local copies, waits for them, and re-layouts: 2.24 us -> none
    pallas_call x1 -> x2, Pallas kernels: 93.4 us -> 95 us  [the longest x1 93.3 us: on_device(): pl.pallas_call(em_kernel, out_shape=results, in_specs=[pl.BlockSpec(memor...]
where the time goes in v2:
time: 95.7 us; the launch traced here: 95.6 us
  Pallas kernels  95 us (99%)
    pallas_call x1, Pallas kernels, on_device(): pl.pallas_call(em_kernel, out_shape=results, in_specs=[pl.BlockSpec(memor...  93.3 us

profile of v2, /device:TPU:0, one launch (start us, length us, event | category | flops | bytes accessed | tf_op | source)
XLA Modules:
  0.0 95.6 jit_solution(4549815837540833498)
XLA Ops:
  0.6 93.3 %shard_map.41 = (f32[256,256]{1,0:T(8,128)}, f32[1,256]{1,0:T(1,128)}) custom-call(f32[512,256]{1,0:T(8,128)} %frames.1, f32[4,2,32,256]{3,2,1,0:T(8,128)} %bitcast.2), custom_call_target="tpu_custom_call" | custom-call | flops 25769803776 | bytes 1048576 | tf_op jit(solution)/shard_map/pallas_call | solution.py:440
  93.9 1.7 %shard_map.42 = (f32[256,256]{1,0:T(8,128)}, f32[1,256]{1,0:T(1,128)}) custom-call(f32[256,256]{1,0:T(8,128)} %get-tuple-element.6.cent, f32[1,256]{1,0:T(1,128)} %get-tuple-element.7.count), custom_call_target="tpu_custom_call" | custom-call | tf_op jit(solution)/shard_map/pallas_call | solution.py:491

commit v3 on v2

--- a/solution.py
+++ b/solution.py
@@ -158,6 +158,7 @@
     for half in range(2):
         for o in range(1, N):
             await_block(0, half, o)
+    forward(2)
 
     def parts_of(codes):
         norms = jnp.sum(codes * codes, axis=1, keepdims=True) * SHARPNESS
@@ -226,14 +227,10 @@
     def move_on(i):
         @pl.when(i == 1)
         def _():
-            forward(2)
-            await_shared(0)
-
-        @pl.when(i == 2)
-        def _():
             forward(3)
             share(1, tok.at[first + before], before)
             share(2, tok.at[first + after], after)
+            await_shared(0)
 
         @pl.when(i == 4)
         def _():

time: 95.7 us -> 98.2 us (1.026)
  Pallas kernels: 95 us -> 97.4 us
    pallas_call x1, Pallas kernels: 93.3 us -> 95.8 us  [on_device(): pl.pallas_call(em_kernel, out_shape=results, in_specs=[pl.BlockSpec(memor...]
where the time goes in v3:
time: 98.2 us; the launch traced here: 98.1 us
  Pallas kernels  97.4 us (99%)
    pallas_call x1, Pallas kernels, on_device(): pl.pallas_call(em_kernel, out_shape=results, in_specs=[pl.BlockSpec(memor...  95.8 us

profile of v3, /device:TPU:0, one launch (start us, length us, event | category | flops | bytes accessed | tf_op | source)
XLA Modules:
  0.0 98.1 jit_solution(10843156252299368516)
XLA Ops:
  0.6 95.8 %shard_map.41 = (f32[256,256]{1,0:T(8,128)}, f32[1,256]{1,0:T(1,128)}) custom-call(f32[512,256]{1,0:T(8,128)} %frames.1, f32[4,2,32,256]{3,2,1,0:T(8,128)} %bitcast.2), custom_call_target="tpu_custom_call" | custom-call | flops 25769803776 | bytes 1048576 | tf_op jit(solution)/shard_map/pallas_call | solution.py:437
  96.4 1.7 %shard_map.42 = (f32[256,256]{1,0:T(8,128)}, f32[1,256]{1,0:T(1,128)}) custom-call(f32[256,256]{1,0:T(8,128)} %get-tuple-element.6.cent, f32[1,256]{1,0:T(1,128)} %get-tuple-element.7.count), custom_call_target="tpu_custom_call" | custom-call | tf_op jit(solution)/shard_map/pallas_call | solution.py:488

commit v4 on v2

--- a/solution.py
+++ b/solution.py
@@ -226,11 +226,11 @@
     def move_on(i):
         @pl.when(i == 1)
         def _():
-            forward(2)
             await_shared(0)
 
         @pl.when(i == 2)
         def _():
+            forward(2)
             forward(3)
             share(1, tok.at[first + before], before)
             share(2, tok.at[first + after], after)

time: 95.7 us -> 95.7 us (level)
  no operation moved by 1% of the time
where the time goes in v4:
time: 95.7 us; the launch traced here: 95.6 us
  Pallas kernels  94.9 us (99%)
    pallas_call x1, Pallas kernels, on_device(): pl.pallas_call(em_kernel, out_shape=results, in_specs=[pl.BlockSpec(memor...  93.3 us

profile of v4, /device:TPU:0, one launch (start us, length us, event | category | flops | bytes accessed | tf_op | source)
XLA Modules:
  0.0 95.6 jit_solution(18443388261091192135)
XLA Ops:
  0.6 93.3 %shard_map.41 = (f32[256,256]{1,0:T(8,128)}, f32[1,256]{1,0:T(1,128)}) custom-call(f32[512,256]{1,0:T(8,128)} %frames.1, f32[4,2,32,256]{3,2,1,0:T(8,128)} %bitcast.2), custom_call_target="tpu_custom_call" | custom-call | flops 25769803776 | bytes 1048576 | tf_op jit(solution)/shard_map/pallas_call | solution.py:440
  93.9 1.7 %shard_map.42 = (f32[256,256]{1,0:T(8,128)}, f32[1,256]{1,0:T(1,128)}) custom-call(f32[256,256]{1,0:T(8,128)} %get-tuple-element.6.cent, f32[1,256]{1,0:T(1,128)} %get-tuple-element.7.count), custom_call_target="tpu_custom_call" | custom-call | tf_op jit(solution)/shard_map/pallas_call | solution.py:491

commit v5 on v4

--- a/solution.py
+++ b/solution.py
@@ -154,7 +154,6 @@
         await_stage1(0, half)
         start_stage2(0, half, (1, 3, 2))
     forward(0)
-    forward(1)
     for half in range(2):
         for o in range(1, N):
             await_block(0, half, o)
@@ -226,6 +225,7 @@
     def move_on(i):
         @pl.when(i == 1)
         def _():
+            forward(1)
             await_shared(0)
 
         @pl.when(i == 2)

time: 95.7 us -> 95.9 us (level)
  no operation moved by 1% of the time
where the time goes in v5:
time: 95.9 us; the launch traced here: 95.7 us
  Pallas kernels  95.1 us (99%)
    pallas_call x1, Pallas kernels, on_device(): pl.pallas_call(em_kernel, out_shape=results, in_specs=[pl.BlockSpec(memor...  93.4 us

profile of v5, /device:TPU:0, one launch (start us, length us, event | category | flops | bytes accessed | tf_op | source)
XLA Modules:
  0.0 95.7 jit_solution(17980962835133080867)
XLA Ops:
  0.6 93.4 %shard_map.41 = (f32[256,256]{1,0:T(8,128)}, f32[1,256]{1,0:T(1,128)}) custom-call(f32[512,256]{1,0:T(8,128)} %frames.1, f32[4,2,32,256]{3,2,1,0:T(8,128)} %bitcast.2), custom_call_target="tpu_custom_call" | custom-call | flops 25769803776 | bytes 1048576 | tf_op jit(solution)/shard_map/pallas_call | solution.py:440
  94.0 1.7 %shard_map.42 = (f32[256,256]{1,0:T(8,128)}, f32[1,256]{1,0:T(1,128)}) custom-call(f32[256,256]{1,0:T(8,128)} %get-tuple-element.6.cent, f32[1,256]{1,0:T(1,128)} %get-tuple-element.7.count), custom_call_target="tpu_custom_call" | custom-call | tf_op jit(solution)/shard_map/pallas_call | solution.py:491
